TPU v7x, 32 devices: a whole 2x2x4 slice. The times are simulated.
32 devices in a mesh: depth: 8 (over z, x), height: 4 (over y, core).
Axes of the slice: x: 2, y: 2, z: 4, core: 2. Of those that a mesh axis runs over, the one named last changes fastest.
Arguments:
- queries: bfloat16 [1792, 512], P('depth', 'height'), may hold values from -6 to 6
- key_vectors: bfloat16 [1792, 512], P('depth', 'height'), may hold values from -6 to 6
- value_vectors: bfloat16 [1792, 512], P('depth', 'height'), may hold values from -6 to 6
- grad_conv: bfloat16 [16, 16, 56, 256], P('depth', 'height'), may hold values from -6 to 6
- conv_weight: bfloat16 [3, 3, 3, 256, 256], replicated, may hold values from -0.078125 to 0.078125
- dec_weight: bfloat16 [512, 8, 256], replicated, may hold values from -0.125 to 0.125
Outputs:
- grad_queries: bfloat16 [1792, 512], P('depth', 'height')
- grad_keys: bfloat16 [1792, 512], P('depth', 'height')
- grad_values: bfloat16 [1792, 512], P('depth', 'height')
All inputs are finite; a program needn't handle non-finite values.
Results may differ from a plain program's by a relative error of at most 0.024.
Values may be sent and summed in bfloat16 or wider, within the bound.
A program may use at most 128 MiB of HBM per device.

v0:
```python
import math

import jax
import jax.numpy as jnp
from jax import lax
from jax.sharding import PartitionSpec as P

HSZ = 64


LOSS_SCALE = 64.0
NEG_START = -1e30


def with_halo(block, sides, width):
    for axis, dim in sides:
        count = lax.axis_size(axis)
        forward = [(i, i + 1) for i in range(count - 1)]
        backward = [(target, source) for source, target in forward]
        low = lax.ppermute(
            lax.slice_in_dim(block, block.shape[dim] - width, None, axis=dim), axis, forward
        )
        high = lax.ppermute(lax.slice_in_dim(block, 0, width, axis=dim), axis, backward)
        block = jnp.concatenate([low, block, high], axis=dim)
    return block


def head_scale():
    return 1.0 / math.sqrt(HSZ)


def block_rows(row_count):
    block_size = min(row_count, 2048)
    while row_count % block_size:
        block_size = block_size - 1
    return block_size


def over_blocks(update, carried, pieces):
    row_count = pieces[0].shape[0]
    block_size = block_rows(row_count)
    if block_size == row_count:
        return update(carried, pieces)
    shaped = tuple(
        (piece.reshape((row_count // block_size, block_size) + piece.shape[1:]) for piece in pieces)
    )

    def advance(current, blocks):
        return (update(current, blocks), None)

    carried, ignored = lax.scan(advance, carried, shaped)
    return carried


def products(left_rows, right_rows):
    left_heads = left_rows.reshape(left_rows.shape[0], -1, HSZ)
    right_heads = right_rows.reshape(right_rows.shape[0], -1, HSZ)
    return jnp.einsum("qhd,khd->hqk", left_heads, right_heads, preferred_element_type=jnp.float32)


def stats_update(queries, grad_rows):

    def update(carried, pieces):
        row_max, denominator, numerator = carried
        key_block, value_block = pieces
        logits = products(queries, key_block) * head_scale()
        new_max = jnp.maximum(row_max, jnp.max(logits, axis=2))
        fading = jnp.exp(row_max - new_max)
        weights = jnp.exp(logits - new_max[:, :, None])
        slopes = products(grad_rows, value_block)
        denominator = denominator * fading + jnp.sum(weights, axis=2)
        numerator = numerator * fading + jnp.sum(weights * slopes, axis=2)
        return (new_max, denominator, numerator)

    return update


def finish_stats(carried):
    row_max, denominator, numerator = carried
    return (row_max + jnp.log(denominator), numerator / denominator)


def softmax_grads(query_rows, grad_rows, log_norm, delta_rows, key_block, value_block):
    logits = products(query_rows, key_block) * head_scale()
    softmax_rows = jnp.exp(logits - log_norm[:, :, None])
    slopes = products(grad_rows, value_block)
    score_grads = (softmax_rows * (slopes - delta_rows[:, :, None])).astype(jnp.bfloat16)
    return (softmax_rows.astype(jnp.bfloat16), score_grads)


def query_term(score_grads, key_block):
    key_heads = key_block.reshape(key_block.shape[0], -1, HSZ)
    result = jnp.einsum("hqk,khd->qhd", score_grads, key_heads, preferred_element_type=jnp.float32)
    return result.reshape(result.shape[0], -1) * head_scale()


def key_term(score_grads, query_rows):
    query_heads = query_rows.reshape(query_rows.shape[0], -1, HSZ)
    result = jnp.einsum(
        "hqk,qhd->khd", score_grads, query_heads, preferred_element_type=jnp.float32
    )
    return result.reshape(result.shape[0], -1) * head_scale()


def value_term(prob_rows, grad_rows):
    grad_heads = grad_rows.reshape(grad_rows.shape[0], -1, HSZ)
    result = jnp.einsum("hqk,qhd->khd", prob_rows, grad_heads, preferred_element_type=jnp.float32)
    return result.reshape(result.shape[0], -1)


def body(queries, key_vectors, value_vectors, grad_conv, conv_weight, dec_weight):
    depth_len, rows_len, cols_len, channels = grad_conv.shape
    padded = with_halo(grad_conv, (("depth", 0), ("height", 1)), 1)
    padded = jnp.pad(padded, ((0, 0), (0, 0), (1, 1), (0, 0)))
    shifted = []
    for along_depth in range(3):
        for along_rows in range(3):
            for along_cols in range(3):
                shifted.append(
                    padded[
                        2 - along_depth : 2 - along_depth + depth_len,
                        2 - along_rows : 2 - along_rows + rows_len,
                        2 - along_cols : 2 - along_cols + cols_len,
                    ]
                )
    stacked = jnp.stack(shifted, axis=3).reshape(depth_len * rows_len * cols_len, 27, channels)
    kernel = conv_weight.reshape(27, channels, channels)
    voxel_grads = lax.dot_general(
        stacked, kernel, (((1, 2), (0, 2)), ((), ())), preferred_element_type=jnp.float32
    )
    voxel_grads = (LOSS_SCALE * voxel_grads).astype(jnp.bfloat16)
    token_rows = rows_len // 2
    token_cols = cols_len // 2
    grouped = voxel_grads.reshape(2, token_rows, 2, token_cols, 2, channels)
    grouped = grouped.transpose(1, 3, 0, 2, 4, 5).reshape(token_rows * token_cols, 8 * channels)
    decoder = dec_weight.reshape(dec_weight.shape[0], 8 * channels)
    out_grads = lax.dot_general(
        grouped, decoder, (((1,), (1,)), ((), ())), preferred_element_type=jnp.float32
    )
    spread = out_grads.astype(jnp.bfloat16).reshape(token_rows, token_cols, decoder.shape[0])
    arranged = lax.all_to_all(spread, "height", split_axis=2, concat_axis=0, tiled=True)
    grad_rows = arranged.reshape(-1, arranged.shape[2])
    tokens_here, width_here = queries.shape
    heads_here = width_here // HSZ
    empty_rows = jnp.zeros((heads_here, tokens_here), jnp.float32)
    start_stats = (
        jnp.full((heads_here, tokens_here), NEG_START, jnp.float32),
        empty_rows,
        empty_rows,
    )
    empty_grads = jnp.zeros((tokens_here, width_here), jnp.float32)
    update = stats_update(queries, grad_rows)
    every_keys, every_values = (
        lax.all_gather(key_vectors, "depth", axis=0, tiled=True),
        lax.all_gather(value_vectors, "depth", axis=0, tiled=True),
    )
    log_norm, delta_rows = finish_stats(
        over_blocks(update, start_stats, (every_keys, every_values))
    )
    every_queries, every_grads = (
        lax.all_gather(queries, "depth", axis=0, tiled=True),
        lax.all_gather(grad_rows, "depth", axis=0, tiled=True),
    )
    every_norms, every_deltas = (
        lax.all_gather(log_norm, "depth", axis=1, tiled=True),
        lax.all_gather(delta_rows, "depth", axis=1, tiled=True),
    )

    def query_update(query_acc, pieces):
        key_block, value_block = pieces
        prob_rows, score_grads = softmax_grads(
            queries, grad_rows, log_norm, delta_rows, key_block, value_block
        )
        return query_acc + query_term(score_grads, key_block)

    query_acc = over_blocks(query_update, empty_grads, (every_keys, every_values))

    def owner_update(carried, pieces):
        key_acc, value_acc = carried
        query_block, grad_block, norm_block, delta_block = pieces
        prob_rows, score_grads = softmax_grads(
            query_block, grad_block, norm_block.T, delta_block.T, key_vectors, value_vectors
        )
        return (
            key_acc + key_term(score_grads, query_block),
            value_acc + value_term(prob_rows, grad_block),
        )

    grad_keys, grad_values = over_blocks(
        owner_update,
        (empty_grads, empty_grads),
        (every_queries, every_grads, every_norms.T, every_deltas.T),
    )
    return (
        query_acc.astype(jnp.bfloat16),
        grad_keys.astype(jnp.bfloat16),
        grad_values.astype(jnp.bfloat16),
    )


def solution(mesh):
    in_specs = (
        P("depth", "height"),
        P("depth", "height"),
        P("depth", "height"),
        P("depth", "height", None, None),
        P(),
        P(),
    )
    out_specs = (P("depth", "height"), P("depth", "height"), P("depth", "height"))
    return jax.shard_map(body, mesh=mesh, in_specs=in_specs, out_specs=out_specs, check_vma=False)
```

profile of v0, /device:TPU:0, one launch (start us, length us, event | category | flops | bytes accessed | tf_op | source)
XLA Modules:
  0.0 280.3 jit_solution(4861210505701734895)
XLA Ops:
  0.6 1.8 fusion.29
  2.5 5.5 %collective-permute-start = (bf16[1,4,56,256]{3,2,1,0:T(8,128)(2,1)}, bf16[1,4,56,256]{3,2,1,0:T(8,128)(2,1)}, u32[]{:S(2)}, u32[]{:S(2)}) collective-permute-start(bf16[1,4,56,256]{3,2,1,0:T(8,128)(2,1)} %get-tuple-element.47), channel_id=1, source_target_pairs={{0,4},{4,8},{8,12},{12,16},{16,20},{20,24},{24,28},{1,5},{5,9},{9,... | collective-permute-start | bytes 344072 | tf_op jit(solution)/shard_map/ppermute | solution.py:20
  9.2 3.6 %copy.53 = bf16[64,8,8,256]{3,1,2,0:T(8,128)(2,1)} copy(bf16[64,8,8,256]{3,2,1,0:T(8,128)(2,1)} %bitcast.93) | data formatting | bytes 4194304
  12.9 35.3 %all_gather.18 = bf16[1792,128]{1,0:T(8,128)(2,1)} all-gather(bf16[224,128]{1,0:T(8,128)(2,1)} %param.7), channel_id=1, replica_groups=mesh['depth'=8,'height'=4] {'depth'}, dimensions={0}, use_global_device_ids=true | all-gather | bytes 516096 | tf_op jit(solution)/shard_map/all_gather | solution.py:154
  48.2 2.0 copy.35
  51.8 3.3 %fusion.30 = (f32[2,224]{1,0:T(2,128)S(1)}, f32[2,224,1792]{2,1,0:T(8,128)}) fusion(bf16[224,2,64]{0,2,1:T(8,128)(2,1)} %bitcast.129, bf16[1792,2,64]{0,2,1:T(8,128)(2,1)} %bitcast.87), kind=kOutput, calls=%fused_computation.85 | convolution fusion | flops 104365632 | bytes 3729152 | tf_op jit(solution)/shard_map/qhd,khd->hqk/dot_general | solution.py:58
  60.8 33.4 %all_gather.20 = bf16[1792,128]{1,0:T(8,128)(2,1)} all-gather(bf16[224,128]{1,0:T(8,128)(2,1)} %param.6), channel_id=1, replica_groups=mesh['depth'=8,'height'=4] {'depth'}, dimensions={0}, use_global_device_ids=true | all-gather | bytes 516096 | tf_op jit(solution)/shard_map/all_gather | solution.py:161
  95.9 2.5 fusion.7
  98.4 1.7 reshape.144
  100.1 1.8 copy.59
  101.9 1.8 reshape.145
  103.7 3.1 %convolution_convert_fusion = bf16[56,512]{1,0:T(8,128)(2,1)} fusion(bf16[56,2048]{1,0:T(8,128)(2,1)} %reshape.145, bf16[512,2048]{1,0:T(8,128)(2,1)} %bitcast.86), kind=kOutput, calls=%fused_computation.22 | convolution fusion | flops 117469184 | bytes 2383872 | tf_op jit(solution)/shard_map/dot_general | solution.py:137
  108.3 1.7 copy.37
  110.0 2.0 reshape.159
  112.0 5.8 %all-to-all-start = ((bf16[4,2,3584]{2,1,0:T(2,128)(2,1)}), bf16[4,2,3584]{2,1,0:T(2,128)(2,1)}, u32[]{:S(2)}, u32[]{:S(2)}) async-start(bf16[4,2,3584]{2,1,0:T(2,128)(2,1)} %reshape.159), calls=%async_computation | async-start | bytes 114688 | tf_op jit(solution)/shard_map/all_to_all | solution.py:141
  117.8 33.5 %all_gather.19 = bf16[1792,128]{1,0:T(8,128)(2,1)} all-gather(bf16[224,128]{1,0:T(8,128)(2,1)} %param.8), channel_id=1, replica_groups=mesh['depth'=8,'height'=4] {'depth'}, dimensions={0}, use_global_device_ids=true | all-gather | bytes 516096 | tf_op jit(solution)/shard_map/all_gather | solution.py:155
  154.4 2.0 copy.40
  156.4 2.0 copy.42
  158.4 2.2 reshape.160
  160.6 1.8 copy.52
  163.8 1.6 reshape_reshape.4
  166.9 4.7 %fusion = (f32[2,224]{1,0:T(2,128)S(1)}, f32[2,224]{1,0:T(2,128)S(1)}, f32[2,224,1792]{2,1,0:T(8,128)}) fusion(f32[2,224,1792]{2,1,0:T(8,128)} %get-tuple-element.51, f32[2,224]{1,0:T(2,128)S(1)} %broadcast_maximum_fusion, bf16[1792,2,64]{0,2,1:T(8,128)(2,1)} %bitcast.95, bf16[224,2,64]{2,1,0:T(2,128)(2,1)} %reshape_reshape.4), kind=kOutput, calls=%fused_computation.6 | convolution fusion | flops 105970816 | bytes 6944000 | tf_op jit(solution)/shard_map/qhd,khd->hqk/dot_general | solution.py:58
  172.7 26.0 %all-gather = f32[8,224,2]{1,2,0:T(2,128)S(1)} all-gather(f32[1,224,2]{1,2,0:T(2,128)S(1)} %bitcast.134), channel_id=1, replica_groups=mesh['depth'=8,'height'=4] {'depth'}, dimensions={0}, use_global_device_ids=true | all-gather | bytes 16128 | tf_op jit(solution)/shard_map/all_gather | solution.py:165
  199.4 33.5 %all_gather.22 = bf16[1792,128]{1,0:T(8,128)(2,1)} all-gather(bf16[224,128]{1,0:T(8,128)(2,1)} %reshape.151), channel_id=1, replica_groups=mesh['depth'=8,'height'=4] {'depth'}, dimensions={0}, use_global_device_ids=true | all-gather | bytes 516096 | tf_op jit(solution)/shard_map/all_gather | solution.py:162
  232.9 2.0 copy.46
  234.9 1.7 subtract_exponential_fusion
  236.6 1.7 copy-done.1
  238.4 2.3 fusion.12
  240.6 1.6 copy.51
  242.2 26.0 %all-gather.1 = f32[8,224,2]{1,2,0:T(2,128)S(1)} all-gather(f32[1,224,2]{1,2,0:T(2,128)S(1)} %bitcast.135), channel_id=1, replica_groups=mesh['depth'=8,'height'=4] {'depth'}, dimensions={0}, use_global_device_ids=true | all-gather | bytes 16128 | tf_op jit(solution)/shard_map/all_gather | solution.py:166
  268.9 3.9 %fusion.10 = bf16[2,224,64]{1,2,0:T(8,128)(2,1)} fusion(bf16[1792,2,64]{0,2,1:T(8,128)(2,1)} %bitcast.92, f32[2,1792,224]{1,2,0:T(8,128)} %copy-done.1, bf16[1792,2,64]{0,2,1:T(8,128)(2,1)} %bitcast.90, bf16[224,2,64]{0,2,1:T(8,128)(2,1)} %bitcast.125, f32[2,1792]{1,0:T(2,128)} %bitcast.132), kind=kOutput, calls=%fused_computation.19 | convolution fusion | flops 207986688 | bytes 4257792 | tf_op jit(solution)/shard_map/hqk,qhd->khd/dot_general | solution.py:99
  274.3 4.4 %fusion.11 = bf16[2,224,64]{1,2,0:T(8,128)(2,1)} fusion(bf16[1792,2,64]{0,2,1:T(8,128)(2,1)} %bitcast.88, f32[2,224,1792]{2,1,0:T(8,128)} %get-tuple-element.52, f32[2,224,1792]{2,1,0:T(8,128)} %get-tuple-element.51, f32[2,224]{1,0:T(2,128)} %get-tuple-element.49, f32[2,224]{1,0:T(2,128)} %copy-done.3), kind=kOutput, calls=%fused_computation.20 | convolution fusion | flops 106029056 | bytes 6942208 | tf_op jit(solution)/shard_map/hqk,khd->qhd/dot_general | solution.py:93
  (65 shorter events, 23.1 us)
Async XLA Ops:
  0.6 95.3 %copy-start = (bf16[3,3,3,256,256]{4,3,2,1,0:T(8,128)(2,1)S(1)}, bf16[3,3,3,256,256]{4,3,2,1,0:T(8,128)(2,1)}, u32[]{:S(2)}) copy-start(bf16[3,3,3,256,256]{4,3,2,1,0:T(8,128)(2,1)} %param.10) | copy-start | bytes 10616836
  2.5 52.7 %collective-permute-start = (bf16[1,4,56,256]{3,2,1,0:T(8,128)(2,1)}, bf16[1,4,56,256]{3,2,1,0:T(8,128)(2,1)}, u32[]{:S(2)}, u32[]{:S(2)}) collective-permute-start(bf16[1,4,56,256]{3,2,1,0:T(8,128)(2,1)} %get-tuple-element.47), channel_id=1, source_target_pairs={{0,4},{4,8},{8,12},{12,16},{16,20},{20,24},{24,28},{1,5},{5,9},{9,... | collective-permute-start | bytes 344072 | tf_op jit(solution)/shard_map/ppermute | solution.py:20
  7.9 48.1 %collective-permute-start.1 = (bf16[1,4,56,256]{3,2,1,0:T(8,128)(2,1)}, bf16[1,4,56,256]{3,2,1,0:T(8,128)(2,1)}, u32[]{:S(2)}, u32[]{:S(2)}) collective-permute-start(bf16[1,4,56,256]{3,2,1,0:T(8,128)(2,1)} %get-tuple-element.46), channel_id=1, source_target_pairs={{4,0},{8,4},{12,8},{16,12},{20,16},{24,20},{28,24},{5,1},{9,5},{13... | collective-permute-start | bytes 344072 | tf_op jit(solution)/shard_map/ppermute | solution.py:23
  58.2 36.0 %collective-permute-start.2 = (bf16[4,1,56,256]{3,2,1,0:T(8,128)(2,1)S(1)}, bf16[4,1,56,256]{3,2,1,0:T(8,128)(2,1)S(1)}, u32[]{:S(2)}, u32[]{:S(2)}) collective-permute-start(bf16[4,1,56,256]{3,2,1,0:T(8,128)(2,1)S(1)} %get-tuple-element.41), channel_id=1, source_target_pairs={{0,1},{1,2},{2,3},{4,5},{5,6},{6,7},{8,9},{9,10},{10,11},{12,13},{... | collective-permute-start | bytes 344072 | tf_op jit(solution)/shard_map/ppermute | solution.py:20
  59.5 34.7 %collective-permute-start.3 = (bf16[4,1,56,256]{3,2,1,0:T(8,128)(2,1)S(1)}, bf16[4,1,56,256]{3,2,1,0:T(8,128)(2,1)S(1)}, u32[]{:S(2)}, u32[]{:S(2)}) collective-permute-start(bf16[4,1,56,256]{3,2,1,0:T(8,128)(2,1)S(1)} %get-tuple-element.42), channel_id=1, source_target_pairs={{1,0},{2,1},{3,2},{5,4},{6,5},{7,6},{9,8},{10,9},{11,10},{13,12},{... | collective-permute-start | bytes 344072 | tf_op jit(solution)/shard_map/ppermute | solution.py:23
  94.6 1.0 copy-start.2
  112.0 46.4 %all-to-all-start = ((bf16[4,2,3584]{2,1,0:T(2,128)(2,1)}), bf16[4,2,3584]{2,1,0:T(2,128)(2,1)}, u32[]{:S(2)}, u32[]{:S(2)}) async-start(bf16[4,2,3584]{2,1,0:T(2,128)(2,1)} %reshape.159), calls=%async_computation | async-start | bytes 114688 | tf_op jit(solution)/shard_map/all_to_all | solution.py:141
  172.2 0.5 copy-start.3
  199.4 42.8 %copy-start.4 = (f32[2,224]{1,0:T(2,128)S(1)}, f32[2,224]{1,0:T(2,128)}, u32[]{:S(2)}) copy-start(f32[2,224]{1,0:T(2,128)} %get-tuple-element.49) | copy-start | bytes 5380
  236.6 1.7 copy-start.1
where the time goes:
time: 282 us; the launch traced here: 280 us
  blocking collectives  188 us (67%)
  local copies, waits for them, and re-layouts  48.3 us (17%)
  matrix products  25.8 us (9%)
  starting transfers between devices  15.1 us (5%)
    all_gather x1, blocking collectives, body(): lax.all_gather(key_vectors, 'depth', axis=0, tiled=True)  35.3 us
    all_gather x1, blocking collectives, body(): lax.all_gather(value_vectors, 'depth', axis=0, tiled=True)  33.5 us
    all_gather x1, blocking collectives, body(): lax.all_gather(grad_rows, 'depth', axis=0, tiled=True)  33.5 us
    all_gather x1, blocking collectives, body(): lax.all_gather(queries, 'depth', axis=0, tiled=True)  33.4 us
    all_gather x1, blocking collectives, body(): lax.all_gather(log_norm, 'depth', axis=1, tiled=True)  26 us
    all_gather x1, blocking collectives, body(): lax.all_gather(delta_rows, 'depth', axis=1, tiled=True)  26 us
    unnamed x48, local copies, waits for them, and re-layouts  22.2 us
    dot_general x3, matrix products, products(): jnp.einsum('qhd,khd->hqk', left_heads, right_heads, preferred_element_typ...  9.71 us
  transfers between devices with their start and end apart: 5, of which 0 were waited for; matrix products, arithmetic and copies ran while one was open for 7% of the time, Pallas kernels for 0%

commit v1 on v0

v1 whole, which is shorter than its diff:
```python
import functools
import math

import jax
import jax.numpy as jnp
from jax import lax
from jax.experimental import pallas as pl
from jax.experimental.pallas import tpu as pltpu
from jax.sharding import PartitionSpec as P

HSZ = 64
LOSS_SCALE = 64.0
MESH = pl.DeviceIdType.MESH
BF = jnp.bfloat16
F32 = jnp.float32
KEYS, VALUES, QUERIES, GRADS = range(4)


def round_up(value, multiple):
    return (value + multiple - 1) // multiple * multiple


def dot_nt(left, right):
    return lax.dot_general(left, right, (((1,), (1,)), ((), ())), preferred_element_type=F32)


def dot_nn(left, right):
    return lax.dot_general(left, right, (((1,), (0,)), ((), ())), preferred_element_type=F32)


def selection(shape, runs):
    row = lax.broadcasted_iota(jnp.int32, shape, 0)
    col = lax.broadcasted_iota(jnp.int32, shape, 1)
    chosen = None
    for first, count, start, step in runs:
        hit = (row >= first) & (row < first + count) & (col == start + step * (row - first))
        chosen = hit if chosen is None else chosen | hit
    return chosen.astype(F32).astype(BF)


def kernel(
    depth, height, inner,
    q_ref, k_ref, v_ref, x_ref, w_hbm, d_hbm,
    dq_ref, dk_ref, dv_ref,
    halo, w_ref, d_ref, voxels, pieces, landed, blocks, stats, probs, dq_acc, dk_acc, dv_acc,
    load_sems, halo_send, halo_recv, swap_send, swap_recv,
    own_send, pair_send, forward_send, block_recv, stat_send, stat_recv,
):
    planes, rows, cols, channels = x_ref.shape
    colp = halo.shape[2]
    tokens, width = q_ref.shape
    heads = width // HSZ
    scale = 1.0 / math.sqrt(HSZ)
    outer = depth // inner
    tok_rows, tok_cols = rows // 2, cols // 2
    toks = tok_rows * tok_cols
    tokp = pieces.shape[1]

    d = lax.axis_index("depth")
    h = lax.axis_index("height")
    z, x = d // inner, d % inner
    other = inner * z + (inner - 1 - x)

    def line(step):
        return ((z + step) % outer) * inner + x

    def across(step):
        return ((z + step) % outer) * inner + (inner - 1 - x)

    load_w = pltpu.make_async_copy(w_hbm, w_ref, load_sems.at[0])
    load_d = pltpu.make_async_copy(d_hbm, d_ref, load_sems.at[1])
    load_w.start()
    load_d.start()

    halo[...] = jnp.zeros_like(halo)
    halo[1 : 1 + planes, 1 : 1 + rows, 0:cols, :] = x_ref[...]

    barrier = pltpu.get_barrier_semaphore()

    def greet(dd, hh):
        pl.semaphore_signal(barrier, inc=1, device_id=(dd, hh), device_id_type=MESH)

    for step in range(1, height):
        greet(d, (h + step) % height)

    def greet_line(step, carry):
        greet(line(step), h)
        return carry

    lax.fori_loop(1, outer, greet_line, 0)
    if inner == 2:
        def greet_across(step, carry):
            greet(across(step), h)
            return carry
        lax.fori_loop(0, outer, greet_across, 0)

    corners = [(dz, dy) for dz in (-1, 1) for dy in (-1, 1)]
    sides = [(dz, 0) for dz in (-1, 1)] + [(0, dy) for dy in (-1, 1)]

    def exists(dz, dy):
        found = None
        for delta, place, extent in ((dz, d, depth), (dy, h, height)):
            if delta:
                here = (place + delta >= 0) & (place + delta < extent)
                found = here if found is None else found & here
        return found

    count = (height - 1) + (outer - 1) + (outer if inner == 2 else 0)
    for dz, dy in corners:
        there = exists(dz, dy)
        count = count + jnp.where(there, 1, 0)

        @pl.when(there)
        def _(dz=dz, dy=dy):
            greet(d + dz, h + dy)

    pl.semaphore_wait(barrier, count)

    def span(delta, extent, receiving):
        if delta == 0:
            return pl.ds(1, extent)
        if receiving:
            return pl.ds(0 if delta > 0 else extent + 1, 1)
        return pl.ds(extent if delta > 0 else 1, 1)

    def halo_copy(index, dz, dy):
        return pltpu.make_async_remote_copy(
            src_ref=halo.at[span(dz, planes, False), span(dy, rows, False)],
            dst_ref=halo.at[span(dz, planes, True), span(dy, rows, True)],
            send_sem=halo_send.at[index],
            recv_sem=halo_recv.at[index],
            device_id=(d + dz, h + dy),
            device_id_type=MESH,
        )

    ways = sides + corners
    for index, (dz, dy) in enumerate(ways):
        @pl.when(exists(dz, dy))
        def _(index=index, dz=dz, dy=dy):
            halo_copy(index, dz, dy).start()

    sources = {KEYS: k_ref, VALUES: v_ref, QUERIES: q_ref}

    def block_copy(array, slot, send_sem, target):
        return pltpu.make_async_remote_copy(
            src_ref=blocks.at[array, slot],
            dst_ref=blocks.at[array, slot],
            send_sem=send_sem,
            recv_sem=block_recv.at[array, slot],
            device_id=(target, h),
            device_id_type=MESH,
        )

    def send_own(array):
        def one(step, carry):
            block_copy(array, d, own_send.at[array, step], line(step)).start()
            return carry
        lax.fori_loop(1, outer, one, 0)
        if inner == 2:
            block_copy(array, d, pair_send.at[array], other).start()

    def forward(array):
        def one(step, carry):
            slot = line(step)
            block_copy(array, slot, forward_send.at[array, step], other).wait_recv()
            if inner == 2:
                block_copy(array, slot, forward_send.at[array, step], other).start()
            return carry
        lax.fori_loop(1, outer, one, 0)

    def wait_across(array):
        def one(step, carry):
            slot = across(step)
            block_copy(array, slot, pair_send.at[array], other).wait_recv()
            return carry
        if inner == 2:
            lax.fori_loop(0, outer, one, 0)

    for array in (KEYS, VALUES, QUERIES):
        blocks[array, d] = sources[array][...]
        send_own(array)

    for index, (dz, dy) in enumerate(ways):
        @pl.when(exists(-dz, -dy))
        def _(index=index, dz=dz, dy=dy):
            halo_copy(index, dz, dy).wait_recv()
    load_w.wait()
    flat = planes * rows * colp
    total = None
    for l in range(3):
        part = None
        for i in range(3):
            for j in range(3):
                window = halo[2 - i : 2 - i + planes, 2 - j : 2 - j + rows].reshape(flat, channels)
                term = dot_nt(window, w_ref[i, j, l])
                part = term if part is None else part + term
        if l != 1:
            part = pltpu.roll(part, (flat - 1) if l == 0 else 1, 0)
        total = part if total is None else total + part
    voxels[...] = (LOSS_SCALE * total).astype(BF).reshape(planes, rows, colp, channels)

    load_d.wait()
    total = None
    for c in range(2):
        part = None
        for a in range(2):
            for b in range(2):
                lhs = jnp.concatenate([voxels[a, 2 * t + b] for t in range(tok_rows)], axis=0)
                term = dot_nt(lhs, d_ref[4 * a + 2 * b + c])
                part = term if part is None else part + term
        if c == 1:
            part = pltpu.roll(part, tok_rows * colp - 1, 0)
        total = part if total is None else total + part
    pick = selection(
        (tokp, tok_rows * colp), [(t * tok_cols, tok_cols, t * colp, 2) for t in range(tok_rows)]
    )
    compact = dot_nn(pick, total.astype(BF)).astype(BF)
    for hh in range(height):
        pieces[hh] = compact[:, hh * width : (hh + 1) * width]

    def swap_copy(step):
        target = (h + step) % height
        return pltpu.make_async_remote_copy(
            src_ref=pieces.at[target],
            dst_ref=landed.at[h],
            send_sem=swap_send.at[step],
            recv_sem=swap_recv.at[step],
            device_id=(d, target),
            device_id_type=MESH,
        )

    for step in range(1, height):
        swap_copy(step).start()
    landed[h] = pieces[h]
    forward(KEYS)
    forward(VALUES)
    for step in range(1, height):
        swap_copy(step).wait_recv()
    spread = selection((tokens, height * tokp), [(s * toks, toks, s * tokp, 1) for s in range(height)])
    g_own = dot_nn(spread, landed[...].reshape(height * tokp, width)).astype(BF)
    blocks[GRADS, d] = g_own
    send_own(GRADS)
    forward(QUERIES)

    wait_across(KEYS)
    wait_across(VALUES)
    lane = lax.broadcasted_iota(jnp.int32, (tokens, width), 1)
    masks = [(lane >= n * HSZ) & (lane < (n + 1) * HSZ) for n in range(heads)]

    def masked(block, factor=1.0):
        wide = block.astype(F32) * factor
        return [jnp.where(mask, wide, 0.0).astype(BF) for mask in masks]

    def merged(parts):
        result = parts[0]
        for n in range(1, heads):
            result = jnp.where(masks[n], parts[n], result)
        return result

    q_heads = masked(q_ref[...], scale)
    g_heads = masked(g_own)

    def max_step(slot, carry):
        keys = blocks[KEYS, slot]
        return tuple(jnp.maximum(carry[n], dot_nt(q_heads[n], keys)) for n in range(heads))

    low = jnp.full((tokens, tokens), -1e30, F32)
    tops = lax.fori_loop(0, depth, max_step, (low,) * heads)
    tops = [jnp.max(top, axis=1, keepdims=True) for top in tops]

    for n in range(heads):
        dq_acc[n] = jnp.zeros((tokens, width), F32)
        dk_acc[n] = jnp.zeros((tokens, width), F32)
        dv_acc[n] = jnp.zeros((tokens, width), F32)

    def sum_step(slot, carry):
        keys = blocks[KEYS, slot]
        values = blocks[VALUES, slot]
        sums = []
        for n in range(heads):
            weights = jnp.exp(dot_nt(q_heads[n], keys) - tops[n])
            rounded = weights.astype(BF)
            probs[slot, n] = rounded
            dq_acc[n] += dot_nn(rounded, values)
            sums.append(carry[n] + weights)
        return tuple(sums)

    sums = lax.fori_loop(0, depth, sum_step, (jnp.zeros((tokens, tokens), F32),) * heads)
    sums = [jnp.sum(total, axis=1, keepdims=True) for total in sums]
    inverse = [1.0 / total for total in sums]
    out = merged([dq_acc[n] * inverse[n] for n in range(heads)])
    product = g_own.astype(F32) * out
    deltas = [jnp.sum(jnp.where(mask, product, 0.0), axis=1, keepdims=True) for mask in masks]
    columns = [tops[n] + jnp.log(sums[n]) for n in range(heads)] + deltas
    table = jnp.zeros((tokens, width), F32)
    for n, column in enumerate(columns):
        table = jnp.where(lane == n, column, table)
    padded = stats.shape[2]
    if padded > tokens:
        table = jnp.concatenate([table, jnp.zeros((padded - tokens, width), F32)], axis=0)
    stats[d] = table.T[: stats.shape[1]]

    def stat_copy(step):
        return pltpu.make_async_remote_copy(
            src_ref=stats.at[d],
            dst_ref=stats.at[d],
            send_sem=stat_send.at[step],
            recv_sem=stat_recv.at[d],
            device_id=((d + step) % depth, h),
            device_id_type=MESH,
        )

    def stat_wait(slot):
        pltpu.make_async_remote_copy(
            src_ref=stats.at[slot],
            dst_ref=stats.at[slot],
            send_sem=stat_send.at[0],
            recv_sem=stat_recv.at[slot],
            device_id=(slot, h),
            device_id_type=MESH,
        ).wait_recv()

    def stat_start(step, carry):
        stat_copy(step).start()
        return carry

    lax.fori_loop(1, depth, stat_start, 0)
    forward(GRADS)

    for n in range(heads):
        dq_acc[n] = jnp.zeros((tokens, width), F32)

    def query_step(slot, carry):
        keys = blocks[KEYS, slot]
        values = blocks[VALUES, slot]
        for n in range(heads):
            slopes = dot_nt(g_heads[n], values)
            score = (probs[slot, n].astype(F32) * (slopes - deltas[n])).astype(BF)
            dq_acc[n] += dot_nn(score, keys)
        return carry

    lax.fori_loop(0, depth, query_step, 0)
    dq_ref[...] = (merged([dq_acc[n] * inverse[n] for n in range(heads)]) * scale).astype(BF)

    k_heads = masked(k_ref[...], scale)
    v_heads = masked(v_ref[...])

    def owner_block(slot):
        queries = blocks[QUERIES, slot]
        grads = blocks[GRADS, slot]
        table = stats[slot]
        for n in range(heads):
            norm = table[n : n + 1, :tokens]
            delta = table[heads + n : heads + n + 1, :tokens]
            weights = jnp.exp(dot_nt(k_heads[n], queries) - norm)
            score = (weights * (dot_nt(v_heads[n], grads) - delta)).astype(BF)
            dk_acc[n] += dot_nn(score, queries)
            dv_acc[n] += dot_nn(weights.astype(BF), grads)

    def line_step(step, carry):
        slot = line(step)

        @pl.when(step > 0)
        def _():
            stat_wait(slot)

        owner_block(slot)
        return carry

    lax.fori_loop(0, outer, line_step, 0)

    def across_step(step, carry):
        slot = across(step)
        block_copy(QUERIES, slot, pair_send.at[QUERIES], other).wait_recv()
        block_copy(GRADS, slot, pair_send.at[GRADS], other).wait_recv()
        stat_wait(slot)
        owner_block(slot)
        return carry

    if inner == 2:
        lax.fori_loop(0, outer, across_step, 0)
    dk_ref[...] = (merged([dk_acc[n] for n in range(heads)]) * scale).astype(BF)
    dv_ref[...] = merged([dv_acc[n] for n in range(heads)]).astype(BF)

    for index, (dz, dy) in enumerate(ways):
        @pl.when(exists(dz, dy))
        def _(index=index, dz=dz, dy=dy):
            halo_copy(index, dz, dy).wait_send()
    for step in range(1, height):
        swap_copy(step).wait_send()

    def drain_line(step, carry):
        for array in range(4):
            block_copy(array, d, own_send.at[array, step], line(step)).wait_send()
            if inner == 2:
                block_copy(array, line(step), forward_send.at[array, step], other).wait_send()
        return carry

    lax.fori_loop(1, outer, drain_line, 0)
    if inner == 2:
        for array in range(4):
            block_copy(array, d, pair_send.at[array], other).wait_send()

    def drain_stats(step, carry):
        stat_copy(step).wait_send()
        return carry

    lax.fori_loop(1, depth, drain_stats, 0)


def body(mesh_sizes, queries, key_vectors, value_vectors, grad_conv, conv_weight, dec_weight):
    depth, height = mesh_sizes
    inner = 2 if depth % 2 == 0 else 1
    outer = depth // inner
    planes, rows, cols, channels = grad_conv.shape
    colp = round_up(cols + 1, 16)
    tokens, width = queries.shape
    heads = width // HSZ
    tokp = round_up((rows // 2) * (cols // 2), 16)
    features = dec_weight.shape[0]
    decoder = dec_weight.transpose(1, 0, 2)
    out = jax.ShapeDtypeStruct((tokens, width), BF)
    vmem = pl.BlockSpec(memory_space=pltpu.VMEM)
    hbm = pl.BlockSpec(memory_space=pl.ANY)
    dma = pltpu.SemaphoreType.DMA
    return pl.pallas_call(
        functools.partial(kernel, depth, height, inner),
        out_shape=(out, out, out),
        in_specs=[vmem, vmem, vmem, vmem, hbm, hbm],
        out_specs=(vmem, vmem, vmem),
        scratch_shapes=[
            pltpu.VMEM((planes + 2, rows + 2, colp, channels), BF),
            pltpu.VMEM(conv_weight.shape, BF),
            pltpu.VMEM((8, features, channels), BF),
            pltpu.VMEM((planes, rows, colp, channels), BF),
            pltpu.VMEM((height, tokp, width), BF),
            pltpu.VMEM((height, tokp, width), BF),
            pltpu.VMEM((4, depth, tokens, width), BF),
            pltpu.VMEM((depth, round_up(2 * heads, 8), round_up(tokens, 128)), F32),
            pltpu.VMEM((depth, heads, tokens, tokens), BF),
            pltpu.VMEM((heads, tokens, width), F32),
            pltpu.VMEM((heads, tokens, width), F32),
            pltpu.VMEM((heads, tokens, width), F32),
            dma((2,)),
            dma((8,)),
            dma((8,)),
            dma((height,)),
            dma((height,)),
            dma((4, outer)),
            dma((4,)),
            dma((4, outer)),
            dma((4, depth)),
            dma((depth,)),
            dma((depth,)),
        ],
        compiler_params=pltpu.CompilerParams(
            collective_id=0, has_side_effects=True, vmem_limit_bytes=58 * 2**20
        ),
        cost_estimate=pl.CostEstimate(
            flops=4 * 10**9, bytes_accessed=8 * 10**6, transcendentals=2 * 10**6
        ),
    )(queries, key_vectors, value_vectors, grad_conv, conv_weight, decoder)


def solution(mesh):
    in_specs = (
        P("depth", "height"),
        P("depth", "height"),
        P("depth", "height"),
        P("depth", "height", None, None),
        P(),
        P(),
    )
    out_specs = (P("depth", "height"), P("depth", "height"), P("depth", "height"))
    sizes = (mesh.shape["depth"], mesh.shape["height"])
    return jax.shard_map(
        functools.partial(body, sizes),
        mesh=mesh,
        in_specs=in_specs,
        out_specs=out_specs,
        check_vma=False,
    )
```

time: 282 us -> 57.3 us (0.20)
  the two profiles are of different devices: /device:TPU:0 before, /device:TPU:14 now
where the time goes in v1:
time: 57.3 us; the launch traced here: 57 us
  Pallas kernels  48.6 us (85%)
  local copies, waits for them, and re-layouts  7.7 us (13%)
  between operations  0.64 us (1%)
    pallas_call x1, Pallas kernels, body(): pl.pallas_call(functools.partial(kernel, depth, height, inner), out_shape...  48.6 us
    unnamed x4, local copies, waits for them, and re-layouts  7.7 us

profile of v1, /device:TPU:14, one launch (start us, length us, event | category | flops | bytes accessed | tf_op | source)
XLA Modules:
  0.0 57.0 jit_solution(6692295007290783923)
XLA Ops:
  0.6 3.4 %copy.11 = bf16[512,8,256]{2,0,1:T(8,128)(2,1)} copy(bf16[512,8,256]{2,1,0:T(8,128)(2,1)} %param.11) | data formatting | bytes 4194304 | tf_op args[5]
  4.0 48.6 %shard_map.85 = (bf16[224,128]{1,0:T(8,128)(2,1)}, bf16[224,128]{1,0:T(8,128)(2,1)}, bf16[224,128]{1,0:T(8,128)(2,1)}) custom-call(bf16[224,128]{1,0:T(8,128)(2,1)} %q_ref.1, bf16[224,128]{1,0:T(8,128)(2,1)} %k_ref.1, bf16[224,128]{1,0:T(8,128)(2,1)} %v_ref.1, bf16[2,4,56,256]{3,2,1,0:T(8,128)(2,1)} %x_ref.1, bf16[3,3,3,256,256]{4,3,2,1,0:T(8,128)(2,1)} %w_hbm.1, ...), custom_call_target="tpu_custom_call" | custom-call | flops 4000000000 | bytes 8000000 | tf_op jit(solution)/shard_map/pallas_call | solution.py:426
  52.7 1.4 %copy.15 = bf16[224,128]{1,0:T(8,128)(2,1)} copy(bf16[224,128]{1,0:T(8,128)(2,1)} %get-tuple-element.6) | data formatting | bytes 114688
  54.1 1.4 %copy.16 = bf16[224,128]{1,0:T(8,128)(2,1)} copy(bf16[224,128]{1,0:T(8,128)(2,1)} %get-tuple-element.7) | data formatting | bytes 114688
  55.5 1.4 %copy.17 = bf16[224,128]{1,0:T(8,128)(2,1)} copy(bf16[224,128]{1,0:T(8,128)(2,1)} %get-tuple-element.8) | data formatting | bytes 114688

commit v2 on v1

v2 whole, which is shorter than its diff:
```python
import functools
import math

import jax
import jax.numpy as jnp
from jax import lax
from jax.experimental import pallas as pl
from jax.experimental.pallas import tpu as pltpu
from jax.sharding import PartitionSpec as P

HSZ = 64
LOSS_SCALE = 64.0
MESH = pl.DeviceIdType.MESH
BF = jnp.bfloat16
F32 = jnp.float32
KEYS, VALUES, QUERIES, GRADS = range(4)


def round_up(value, multiple):
    return (value + multiple - 1) // multiple * multiple


def dot_nt(left, right):
    return lax.dot_general(left, right, (((1,), (1,)), ((), ())), preferred_element_type=F32)


def dot_nn(left, right):
    return lax.dot_general(left, right, (((1,), (0,)), ((), ())), preferred_element_type=F32)


def selection(shape, runs):
    row = lax.broadcasted_iota(jnp.int32, shape, 0)
    col = lax.broadcasted_iota(jnp.int32, shape, 1)
    chosen = None
    for first, count, start, step in runs:
        hit = (row >= first) & (row < first + count) & (col == start + step * (row - first))
        chosen = hit if chosen is None else chosen | hit
    return chosen.astype(F32).astype(BF)


def kernel(
    depth, height,
    q_ref, k_ref, v_ref, x_ref, w_hbm, d_hbm,
    dq_ref, dk_ref, dv_ref,
    halo, w_ref, d_raw, d_tall, d_ref, voxels, pieces, landed, swapped, blocks, stats, probs,
    acc, results, returned,
    load_sems, halo_send, halo_recv, piece_send, piece_recv, swap_send, swap_recv,
    own_send, block_recv, stat_send, stat_recv, return_send, return_recv,
):
    planes, rows, cols, channels = x_ref.shape
    colp = halo.shape[2]
    tokens, width = q_ref.shape
    scale = 1.0 / math.sqrt(HSZ)
    outer = depth // 2
    tok_rows, tok_cols = rows // 2, cols // 2
    toks = tok_rows * tok_cols
    tokp = pieces.shape[1]

    d = lax.axis_index("depth")
    h = lax.axis_index("height")
    z, x = d // 2, d % 2
    other = 2 * z + (1 - x)

    load_w = pltpu.make_async_copy(w_hbm, w_ref, load_sems.at[0])
    load_d = pltpu.make_async_copy(d_hbm, d_raw, load_sems.at[1])
    load_w.start()
    load_d.start()

    halo[...] = jnp.zeros_like(halo)
    halo[1 : 1 + planes, 1 : 1 + rows, 0:cols, :] = x_ref[...]

    barrier = pltpu.get_barrier_semaphore()

    def greet(dd, hh):
        pl.semaphore_signal(barrier, inc=1, device_id=(dd, hh), device_id_type=MESH)

    def peer(step):
        return ((z + step) % outer) * 2 + x

    greet(other, h)
    for step in range(1, height):
        greet(d, (h + step) % height)
        greet(other, (h + step) % height)

    def greet_line(step, carry):
        greet(peer(step), h)
        return carry

    lax.fori_loop(1, outer, greet_line, 0)
    corners = [(dz, dy) for dz in (-1, 1) for dy in (-1, 1)]
    ways = [(dz, 0) for dz in (-1, 1)] + [(0, dy) for dy in (-1, 1)] + corners

    def exists(dz, dy):
        found = None
        for delta, place, extent in ((dz, d, depth), (dy, h, height)):
            if delta:
                here = (place + delta >= 0) & (place + delta < extent)
                found = here if found is None else found & here
        return found

    count = 1 + 2 * (height - 1) + (outer - 1)
    for dz, dy in ways:
        if dz == 0:
            continue
        there = exists(dz, dy)
        count = count + jnp.where(there, 1, 0)

        @pl.when(there)
        def _(dz=dz, dy=dy):
            greet(d + dz, h + dy)

    pl.semaphore_wait(barrier, count)

    def span(delta, extent, receiving):
        if delta == 0:
            return pl.ds(1, extent)
        if receiving:
            return pl.ds(0 if delta > 0 else extent + 1, 1)
        return pl.ds(extent if delta > 0 else 1, 1)

    def halo_copy(index, dz, dy):
        return pltpu.make_async_remote_copy(
            src_ref=halo.at[span(dz, planes, False), span(dy, rows, False)],
            dst_ref=halo.at[span(dz, planes, True), span(dy, rows, True)],
            send_sem=halo_send.at[index],
            recv_sem=halo_recv.at[index],
            device_id=(d + dz, h + dy),
            device_id_type=MESH,
        )

    def pair_copy(source, target, send_sem, recv_sem):
        return pltpu.make_async_remote_copy(
            src_ref=source,
            dst_ref=target,
            send_sem=send_sem,
            recv_sem=recv_sem,
            device_id=(other, h),
            device_id_type=MESH,
        )

    def swap_copy(array):
        return pair_copy(
            sources[array], swapped.at[array], swap_send.at[array], swap_recv.at[array]
        )

    sources = {KEYS: k_ref, VALUES: v_ref, QUERIES: q_ref}
    swap_copy(KEYS).start()
    for index, (dz, dy) in enumerate(ways):
        @pl.when(exists(dz, dy))
        def _(index=index, dz=dz, dy=dy):
            halo_copy(index, dz, dy).start()
    swap_copy(VALUES).start()
    swap_copy(QUERIES).start()

    lane = lax.broadcasted_iota(jnp.int32, (tokens, width), 1)
    tall_lane = lax.broadcasted_iota(jnp.int32, (2 * tokens, width), 1)
    halves = [lane < HSZ, lane >= HSZ]
    tall_halves = [tall_lane < HSZ, tall_lane >= HSZ]
    mine = (lane >= x * HSZ) & (lane < (x + 1) * HSZ)

    def turned(value):
        return pltpu.roll(value, HSZ, 1)

    def merged(own, received):
        return jnp.where(mine, own.astype(F32), turned(received.astype(F32))).astype(BF)

    def block_copy(array, step):
        return pltpu.make_async_remote_copy(
            src_ref=blocks.at[array, z],
            dst_ref=blocks.at[array, z],
            send_sem=own_send.at[array, step],
            recv_sem=block_recv.at[array, z],
            device_id=(peer(step), h),
            device_id_type=MESH,
        )

    def block_wait(array, slot):
        pltpu.make_async_remote_copy(
            src_ref=blocks.at[array, slot],
            dst_ref=blocks.at[array, slot],
            send_sem=own_send.at[array, 0],
            recv_sem=block_recv.at[array, slot],
            device_id=(other, h),
            device_id_type=MESH,
        ).wait_recv()

    def send_own(array):
        def one(step, carry):
            block_copy(array, step).start()
            return carry
        lax.fori_loop(1, outer, one, 0)

    def wait_all(array):
        def one(step, carry):
            block_wait(array, (z + step) % outer)
            return carry
        lax.fori_loop(1, outer, one, 0)

    load_d.wait()
    features = d_raw.shape[0]
    part_len = d_tall.shape[1] // 8
    for start in range(0, features, part_len):
        wide = d_raw[start : start + part_len].astype(F32).reshape(part_len * 8, channels)
        for lanes in range(d_tall.shape[0]):
            d_tall[lanes] = wide[:, lanes * 128 : (lanes + 1) * 128]
        for s in range(8):
            for lanes in range(d_tall.shape[0]):
                d_ref[s, start : start + part_len, lanes * 128 : (lanes + 1) * 128] = d_tall[
                    lanes, pl.ds(s, part_len, stride=8), :
                ].astype(BF)

    for array in (KEYS, VALUES, QUERIES):
        swap_copy(array).wait_recv()
        blocks[array, z] = merged(sources[array][...], swapped[array])
        send_own(array)

    for index, (dz, dy) in enumerate(ways):
        @pl.when(exists(-dz, -dy))
        def _(index=index, dz=dz, dy=dy):
            halo_copy(index, dz, dy).wait_recv()
    load_w.wait()
    flat = planes * rows * colp
    total = None
    for l in range(3):
        part = None
        for i in range(3):
            for j in range(3):
                window = halo[2 - i : 2 - i + planes, 2 - j : 2 - j + rows].reshape(flat, channels)
                term = dot_nt(window, w_ref[i, j, l])
                part = term if part is None else part + term
        if l != 1:
            part = pltpu.roll(part, (flat - 1) if l == 0 else 1, 0)
        total = part if total is None else total + part
    voxels[...] = (LOSS_SCALE * total).astype(BF).reshape(planes, rows, colp, channels)

    total = None
    for c in range(2):
        part = None
        for a in range(2):
            for b in range(2):
                lhs = jnp.concatenate([voxels[a, 2 * t + b] for t in range(tok_rows)], axis=0)
                term = dot_nt(lhs, d_ref[4 * a + 2 * b + c])
                part = term if part is None else part + term
        if c == 1:
            part = pltpu.roll(part, tok_rows * colp - 1, 0)
        total = part if total is None else total + part
    pick = selection(
        (tokp, tok_rows * colp), [(t * tok_cols, tok_cols, t * colp, 2) for t in range(tok_rows)]
    )
    compact = dot_nn(pick, total.astype(BF)).astype(BF)
    for hh in range(height):
        pieces[hh] = compact[:, hh * width : (hh + 1) * width]

    def piece_copy(away, step):
        target = (h + step) % height
        return pltpu.make_async_remote_copy(
            src_ref=pieces.at[target],
            dst_ref=landed.at[away, h],
            send_sem=piece_send.at[away, step],
            recv_sem=piece_recv.at[away, h],
            device_id=(other if away else d, target),
            device_id_type=MESH,
        )

    def piece_wait(away, slot):
        pltpu.make_async_remote_copy(
            src_ref=landed.at[away, slot],
            dst_ref=landed.at[away, slot],
            send_sem=piece_send.at[away, 0],
            recv_sem=piece_recv.at[away, slot],
            device_id=(other, h),
            device_id_type=MESH,
        ).wait_recv()

    for step in range(height):
        if step:
            piece_copy(0, step).start()
        piece_copy(1, step).start()
    landed[0, h] = pieces[h]

    def placed(block):
        wide = block.astype(F32)
        low = [jnp.where(half, wide, 0.0) for half in halves]
        return [
            jnp.concatenate([low[0], turned(low[1])], axis=0).astype(BF),
            jnp.concatenate([turned(low[0]), low[1]], axis=0).astype(BF),
        ]

    def joined():
        return acc[0] + turned(acc[1])

    def clear(which):
        for f in range(2):
            which[f] = jnp.zeros((2 * tokens, width), F32)

    q_rows = [(part.astype(F32) * scale).astype(BF) for part in placed(blocks[QUERIES, z])]

    for step in range(1, height):
        piece_wait(0, (h + step) % height)
    for step in range(height):
        piece_wait(1, (h + step) % height)
    spread = selection((tokens, height * tokp), [(s * toks, toks, s * tokp, 1) for s in range(height)])
    near, far = [
        dot_nn(spread, landed[away].reshape(height * tokp, width)) for away in range(2)
    ]
    blocks[GRADS, z] = jnp.where(mine, near, turned(far)).astype(BF)
    send_own(GRADS)
    g_rows = placed(blocks[GRADS, z])

    def max_step(step, carry):
        slot = (z + step) % outer

        @pl.when(step > 0)
        def _():
            block_wait(KEYS, slot)

        keys = blocks[KEYS, slot]
        return jnp.maximum(carry, jnp.maximum(dot_nt(q_rows[0], keys), dot_nt(q_rows[1], keys)))

    top = lax.fori_loop(0, outer, max_step, jnp.full((2 * tokens, tokens), -1e30, F32))
    top = jnp.max(top, axis=1, keepdims=True)
    clear(acc)

    def sum_step(step, carry):
        slot = (z + step) % outer

        @pl.when(step > 0)
        def _():
            block_wait(VALUES, slot)

        keys = blocks[KEYS, slot]
        values = blocks[VALUES, slot].astype(F32)
        for f in range(2):
            weights = jnp.exp(dot_nt(q_rows[f], keys) - top).astype(BF)
            probs[slot, f] = weights
            acc[f] += dot_nn(weights, jnp.where(halves[f], values, 1.0).astype(BF))
        return carry

    lax.fori_loop(0, outer, sum_step, 0)
    both = joined()
    sums = turned(both)[:, 0:1]
    inverse = 1.0 / sums
    product = jnp.where(tall_halves[0], both * inverse, 0.0) * g_rows[0].astype(F32)
    delta = jnp.sum(product, axis=1, keepdims=True)
    norm = top + jnp.log(sums)
    columns = [norm[:tokens], norm[tokens:], delta[:tokens], delta[tokens:]]
    table = jnp.zeros((tokens, width), F32)
    for n, column in enumerate(columns):
        table = jnp.where(lane == n, column, table)
    padded = stats.shape[2]
    if padded > tokens:
        table = jnp.concatenate([table, jnp.zeros((padded - tokens, width), F32)], axis=0)
    stats[z] = table.T[: stats.shape[1]]

    def stat_copy(step):
        return pltpu.make_async_remote_copy(
            src_ref=stats.at[z],
            dst_ref=stats.at[z],
            send_sem=stat_send.at[step],
            recv_sem=stat_recv.at[z],
            device_id=(peer(step), h),
            device_id_type=MESH,
        )

    def stat_wait(slot):
        pltpu.make_async_remote_copy(
            src_ref=stats.at[slot],
            dst_ref=stats.at[slot],
            send_sem=stat_send.at[0],
            recv_sem=stat_recv.at[slot],
            device_id=(other, h),
            device_id_type=MESH,
        ).wait_recv()

    def stat_start(step, carry):
        stat_copy(step).start()
        return carry

    lax.fori_loop(1, outer, stat_start, 0)

    def return_copy(index):
        return pair_copy(
            results.at[index], returned.at[index], return_send.at[index], return_recv.at[index]
        )

    def give_back(index, value):
        results[index] = jnp.where(halves[0], value[:tokens], turned(value[tokens:])).astype(BF)
        return_copy(index).start()

    clear(acc)

    def query_step(slot, carry):
        keys = blocks[KEYS, slot]
        values = blocks[VALUES, slot]
        for f in range(2):
            slopes = dot_nt(g_rows[f], values)
            score = (probs[slot, f].astype(F32) * (slopes - delta)).astype(BF)
            acc[f] += dot_nn(score, keys)
        return carry

    lax.fori_loop(0, outer, query_step, 0)
    give_back(0, joined() * (inverse * scale))

    k_rows = [(part.astype(F32) * scale).astype(BF) for part in placed(blocks[KEYS, z])]
    v_rows = placed(blocks[VALUES, z])
    for n in range(4):
        acc[n] = jnp.zeros((2 * tokens, width), F32)

    def owner_step(step, carry):
        slot = (z + step) % outer

        @pl.when(step > 0)
        def _():
            block_wait(QUERIES, slot)
            stat_wait(slot)
            block_wait(GRADS, slot)

        queries = blocks[QUERIES, slot]
        grads = blocks[GRADS, slot]
        table = stats[slot]
        for f in range(2):
            weights = jnp.exp(dot_nt(k_rows[f], queries) - table[f : f + 1, :tokens])
            slopes = dot_nt(v_rows[f], grads) - table[2 + f : 3 + f, :tokens]
            acc[f] += dot_nn((weights * slopes).astype(BF), queries)
            acc[2 + f] += dot_nn(weights.astype(BF), grads)
        return carry

    lax.fori_loop(0, outer, owner_step, 0)
    give_back(1, joined() * scale)
    give_back(2, acc[2] + turned(acc[3]))
    for index, out in enumerate((dq_ref, dk_ref, dv_ref)):
        return_copy(index).wait_recv()
        out[...] = merged(results[index], returned[index])

    for index in range(3):
        return_copy(index).wait_send()
        swap_copy(index).wait_send()
    for index, (dz, dy) in enumerate(ways):
        @pl.when(exists(dz, dy))
        def _(index=index, dz=dz, dy=dy):
            halo_copy(index, dz, dy).wait_send()
    for step in range(height):
        if step:
            piece_copy(0, step).wait_send()
        piece_copy(1, step).wait_send()

    def drain(step, carry):
        for array in range(4):
            block_copy(array, step).wait_send()
        stat_copy(step).wait_send()
        return carry

    lax.fori_loop(1, outer, drain, 0)


def hand_over(a_ref, b_ref, c_ref, a_out, b_out, c_out):
    a_out[...] = a_ref[...]
    b_out[...] = b_ref[...]
    c_out[...] = c_ref[...]


def body(mesh_sizes, queries, key_vectors, value_vectors, grad_conv, conv_weight, dec_weight):
    depth, height = mesh_sizes
    outer = depth // 2
    planes, rows, cols, channels = grad_conv.shape
    colp = round_up(cols + 1, 16)
    tokens, width = queries.shape
    assert depth % 2 == 0 and width == 2 * HSZ
    tokp = round_up((rows // 2) * (cols // 2), 16)
    features = dec_weight.shape[0]
    out = jax.ShapeDtypeStruct((tokens, width), BF)
    vmem = pl.BlockSpec(memory_space=pltpu.VMEM)
    hbm = pl.BlockSpec(memory_space=pl.ANY)
    dma = pltpu.SemaphoreType.DMA
    results = pl.pallas_call(
        functools.partial(kernel, depth, height),
        out_shape=(out, out, out),
        in_specs=[vmem, vmem, vmem, vmem, hbm, hbm],
        out_specs=(vmem, vmem, vmem),
        scratch_shapes=[
            pltpu.VMEM((planes + 2, rows + 2, colp, channels), BF),
            pltpu.VMEM(conv_weight.shape, BF),
            pltpu.VMEM(dec_weight.shape, BF),
            pltpu.VMEM((channels // 128, 512, 128), F32),
            pltpu.VMEM((8, features, channels), BF),
            pltpu.VMEM((planes, rows, colp, channels), BF),
            pltpu.VMEM((height, tokp, width), BF),
            pltpu.VMEM((2, height, tokp, width), BF),
            pltpu.VMEM((3, tokens, width), BF),
            pltpu.VMEM((4, outer, tokens, width), BF),
            pltpu.VMEM((outer, 8, round_up(tokens, 128)), F32),
            pltpu.VMEM((outer, 2, 2 * tokens, tokens), BF),
            pltpu.VMEM((4, 2 * tokens, width), F32),
            pltpu.VMEM((3, tokens, width), BF),
            pltpu.VMEM((3, tokens, width), BF),
            dma((2,)),
            dma((8,)),
            dma((8,)),
            dma((2, height)),
            dma((2, height)),
            dma((3,)),
            dma((3,)),
            dma((4, outer)),
            dma((4, outer)),
            dma((outer,)),
            dma((outer,)),
            dma((3,)),
            dma((3,)),
        ],
        compiler_params=pltpu.CompilerParams(
            collective_id=0, has_side_effects=True, vmem_limit_bytes=58 * 2**20
        ),
        cost_estimate=pl.CostEstimate(
            flops=4 * 10**9, bytes_accessed=8 * 10**6, transcendentals=2 * 10**6
        ),
    )(queries, key_vectors, value_vectors, grad_conv, conv_weight, dec_weight)
    return pl.pallas_call(
        hand_over,
        out_shape=(out, out, out),
        in_specs=[vmem, vmem, vmem],
        out_specs=(vmem, vmem, vmem),
    )(*results)


def solution(mesh):
    in_specs = (
        P("depth", "height"),
        P("depth", "height"),
        P("depth", "height"),
        P("depth", "height", None, None),
        P(),
        P(),
    )
    out_specs = (P("depth", "height"), P("depth", "height"), P("depth", "height"))
    sizes = (mesh.shape["depth"], mesh.shape["height"])
    return jax.shard_map(
        functools.partial(body, sizes),
        mesh=mesh,
        in_specs=in_specs,
        out_specs=out_specs,
        check_vma=False,
    )
```

time: 57.3 us -> 46 us (0.80)
  the two profiles are of different devices: /device:TPU:14 before, /device:TPU:0 now
where the time goes in v2:
time: 46 us; the launch traced here: 45.9 us
  Pallas kernels  45.2 us (98%)
  between operations  0.64 us (1%)
    pallas_call x1, Pallas kernels, body(): pl.pallas_call(functools.partial(kernel, depth, height), out_shape=(out,...  43.7 us
    pallas_call x1, Pallas kernels, body(): pl.pallas_call(hand_over, out_shape=(out, out, out), in_specs=[vmem, vmem...  1.54 us

profile of v2, /device:TPU:0, one launch (start us, length us, event | category | flops | bytes accessed | tf_op | source)
XLA Modules:
  0.0 45.9 jit_solution(16933844184058459255)
XLA Ops:
  0.6 43.7 %shard_map.85 = (bf16[224,128]{1,0:T(8,128)(2,1)}, bf16[224,128]{1,0:T(8,128)(2,1)}, bf16[224,128]{1,0:T(8,128)(2,1)}) custom-call(bf16[224,128]{1,0:T(8,128)(2,1)} %q_ref.1, bf16[224,128]{1,0:T(8,128)(2,1)} %k_ref.1, bf16[224,128]{1,0:T(8,128)(2,1)} %v_ref.1, bf16[2,4,56,256]{3,2,1,0:T(8,128)(2,1)} %x_ref.1, bf16[3,3,3,256,256]{4,3,2,1,0:T(8,128)(2,1)} %w_hbm.1, ...), custom_call_target="tpu_custom_call" | custom-call | flops 4000000000 | bytes 8000000 | tf_op jit(solution)/shard_map/pallas_call | solution.py:475
  44.3 1.5 %shard_map.86 = (bf16[224,128]{1,0:T(8,128)(2,1)}, bf16[224,128]{1,0:T(8,128)(2,1)}, bf16[224,128]{1,0:T(8,128)(2,1)}) custom-call(bf16[224,128]{1,0:T(8,128)(2,1)} %get-tuple-element.6.a_ref, bf16[224,128]{1,0:T(8,128)(2,1)} %get-tuple-element.7.b_ref, bf16[224,128]{1,0:T(8,128)(2,1)} %get-tuple-element.8.c_ref), custom_call_target="tpu_custom_call" | custom-call | tf_op jit(solution)/shard_map/pallas_call | solution.py:517

commit v3 on v2

--- a/solution.py
+++ b/solution.py
@@ -42,7 +42,7 @@
     depth, height,
     q_ref, k_ref, v_ref, x_ref, w_hbm, d_hbm,
     dq_ref, dk_ref, dv_ref,
-    halo, w_ref, d_raw, d_tall, d_ref, voxels, pieces, landed, swapped, blocks, stats, probs,
+    halo, w_ref, d_raw, d_tall, d_ref, windows, voxels, pieces, landed, swapped, blocks, stats, probs,
     acc, results, returned,
     load_sems, halo_send, halo_recv, piece_send, piece_recv, swap_send, swap_recv,
     own_send, block_recv, stat_send, stat_recv, return_send, return_recv,
@@ -52,6 +52,7 @@
     tokens, width = q_ref.shape
     scale = 1.0 / math.sqrt(HSZ)
     outer = depth // 2
+    groups, chunk = probs.shape[0], outer // probs.shape[0]
     tok_rows, tok_cols = rows // 2, cols // 2
     toks = tok_rows * tok_cols
     tokp = pieces.shape[1]
@@ -61,10 +62,21 @@
     z, x = d // 2, d % 2
     other = 2 * z + (1 - x)
 
-    load_w = pltpu.make_async_copy(w_hbm, w_ref, load_sems.at[0])
-    load_d = pltpu.make_async_copy(d_hbm, d_raw, load_sems.at[1])
-    load_w.start()
+    taps = [(i, j) for i in range(3) for j in range(3)]
+    load_d = pltpu.make_async_copy(d_hbm, d_raw, load_sems.at[27])
     load_d.start()
+    loads_w = []
+    for n, (i, j) in enumerate(taps):
+        for l in range(3):
+            loads_w.append(
+                pltpu.make_async_copy(
+                    w_hbm.at[i, j, l],
+                    w_ref.at[pl.ds(l * channels, channels), pl.ds(n * channels, channels)],
+                    load_sems.at[3 * n + l],
+                )
+            )
+    for load in loads_w:
+        load.start()
 
     halo[...] = jnp.zeros_like(halo)
     halo[1 : 1 + planes, 1 : 1 + rows, 0:cols, :] = x_ref[...]
@@ -205,7 +217,8 @@
             d_tall[lanes] = wide[:, lanes * 128 : (lanes + 1) * 128]
         for s in range(8):
             for lanes in range(d_tall.shape[0]):
-                d_ref[s, start : start + part_len, lanes * 128 : (lanes + 1) * 128] = d_tall[
+                place = (s // 2) * channels + lanes * 128
+                d_ref[s % 2, start : start + part_len, place : place + 128] = d_tall[
                     lanes, pl.ds(s, part_len, stride=8), :
                 ].astype(BF)
 
@@ -218,32 +231,30 @@
         @pl.when(exists(-dz, -dy))
         def _(index=index, dz=dz, dy=dy):
             halo_copy(index, dz, dy).wait_recv()
-    load_w.wait()
+    for load in loads_w:
+        load.wait()
     flat = planes * rows * colp
-    total = None
-    for l in range(3):
-        part = None
-        for i in range(3):
-            for j in range(3):
-                window = halo[2 - i : 2 - i + planes, 2 - j : 2 - j + rows].reshape(flat, channels)
-                term = dot_nt(window, w_ref[i, j, l])
-                part = term if part is None else part + term
-        if l != 1:
-            part = pltpu.roll(part, (flat - 1) if l == 0 else 1, 0)
-        total = part if total is None else total + part
+    for n, (i, j) in enumerate(taps):
+        window = halo[2 - i : 2 - i + planes, 2 - j : 2 - j + rows]
+        windows[:, n * channels : (n + 1) * channels] = window.reshape(flat, channels)
+    sums = dot_nt(windows[...], w_ref[...])
+    total = (
+        pltpu.roll(sums[:, :channels], flat - 1, 0)
+        + sums[:, channels : 2 * channels]
+        + pltpu.roll(sums[:, 2 * channels :], 1, 0)
+    )
     voxels[...] = (LOSS_SCALE * total).astype(BF).reshape(planes, rows, colp, channels)
 
-    total = None
-    for c in range(2):
-        part = None
-        for a in range(2):
-            for b in range(2):
-                lhs = jnp.concatenate([voxels[a, 2 * t + b] for t in range(tok_rows)], axis=0)
-                term = dot_nt(lhs, d_ref[4 * a + 2 * b + c])
-                part = term if part is None else part + term
-        if c == 1:
-            part = pltpu.roll(part, tok_rows * colp - 1, 0)
-        total = part if total is None else total + part
+    lhs = jnp.concatenate(
+        [
+            jnp.concatenate([voxels[a, 2 * t + b] for t in range(tok_rows)], axis=0)
+            for a in range(2)
+            for b in range(2)
+        ],
+        axis=1,
+    )
+    parts = [dot_nt(lhs, d_ref[c]) for c in range(2)]
+    total = parts[0] + pltpu.roll(parts[1], tok_rows * colp - 1, 0)
     pick = selection(
         (tokp, tok_rows * colp), [(t * tok_cols, tok_cols, t * colp, 2) for t in range(tok_rows)]
     )
@@ -307,36 +318,47 @@
     send_own(GRADS)
     g_rows = placed(blocks[GRADS, z])
 
-    def max_step(step, carry):
-        slot = (z + step) % outer
-
-        @pl.when(step > 0)
-        def _():
-            block_wait(KEYS, slot)
-
-        keys = blocks[KEYS, slot]
-        return jnp.maximum(carry, jnp.maximum(dot_nt(q_rows[0], keys), dot_nt(q_rows[1], keys)))
-
-    top = lax.fori_loop(0, outer, max_step, jnp.full((2 * tokens, tokens), -1e30, F32))
-    top = jnp.max(top, axis=1, keepdims=True)
-    clear(acc)
-
-    def sum_step(step, carry):
-        slot = (z + step) % outer
-
-        @pl.when(step > 0)
-        def _():
-            block_wait(VALUES, slot)
-
-        keys = blocks[KEYS, slot]
-        values = blocks[VALUES, slot].astype(F32)
+    def span_of(array, group):
+        part = blocks[array, pl.ds(group * chunk, chunk)]
+        return part.reshape(chunk * tokens, width)
+
+    def logits(group):
+        keys = span_of(KEYS, group)
+        return [dot_nt(q_rows[f], keys) for f in range(2)]
+
+    def highest(values):
+        return jnp.max(jnp.maximum(values[0], values[1]), axis=1, keepdims=True)
+
+    long_lane = lax.broadcasted_iota(jnp.int32, (chunk * tokens, width), 1)
+    long_halves = [long_lane < HSZ, long_lane >= HSZ]
+
+    def accumulate(group, values, first):
+        held = span_of(VALUES, group).astype(F32)
         for f in range(2):
-            weights = jnp.exp(dot_nt(q_rows[f], keys) - top).astype(BF)
-            probs[slot, f] = weights
-            acc[f] += dot_nn(weights, jnp.where(halves[f], values, 1.0).astype(BF))
-        return carry
-
-    lax.fori_loop(0, outer, sum_step, 0)
+            weights = jnp.exp(values[f] - top).astype(BF)
+            probs[group, f] = weights
+            term = dot_nn(weights, jnp.where(long_halves[f], held, 1.0).astype(BF))
+            acc[f] = term if first else acc[f] + term
+
+    wait_all(KEYS)
+    if groups == 1:
+        values = logits(0)
+        top = highest(values)
+        wait_all(VALUES)
+        accumulate(0, values, True)
+    else:
+        def max_step(group, carry):
+            return jnp.maximum(carry, highest(logits(group)))
+
+        top = lax.fori_loop(0, groups, max_step, jnp.full((2 * tokens, 1), -1e30, F32))
+        wait_all(VALUES)
+        clear(acc)
+
+        def sum_step(group, carry):
+            accumulate(group, logits(group), False)
+            return carry
+
+        lax.fori_loop(0, groups, sum_step, 0)
     both = joined()
     sums = turned(both)[:, 0:1]
     inverse = 1.0 / sums
@@ -387,18 +409,25 @@
         results[index] = jnp.where(halves[0], value[:tokens], turned(value[tokens:])).astype(BF)
         return_copy(index).start()
 
-    clear(acc)
-
-    def query_step(slot, carry):
-        keys = blocks[KEYS, slot]
-        values = blocks[VALUES, slot]
+    def query_block(group, first):
+        keys = span_of(KEYS, group)
+        held = span_of(VALUES, group)
         for f in range(2):
-            slopes = dot_nt(g_rows[f], values)
-            score = (probs[slot, f].astype(F32) * (slopes - delta)).astype(BF)
-            acc[f] += dot_nn(score, keys)
-        return carry
-
-    lax.fori_loop(0, outer, query_step, 0)
+            slopes = dot_nt(g_rows[f], held)
+            score = (probs[group, f].astype(F32) * (slopes - delta)).astype(BF)
+            term = dot_nn(score, keys)
+            acc[f] = term if first else acc[f] + term
+
+    if groups == 1:
+        query_block(0, True)
+    else:
+        clear(acc)
+
+        def query_step(group, carry):
+            query_block(group, False)
+            return carry
+
+        lax.fori_loop(0, groups, query_step, 0)
     give_back(0, joined() * (inverse * scale))
 
     k_rows = [(part.astype(F32) * scale).astype(BF) for part in placed(blocks[KEYS, z])]
@@ -468,6 +497,7 @@
     assert depth % 2 == 0 and width == 2 * HSZ
     tokp = round_up((rows // 2) * (cols // 2), 16)
     features = dec_weight.shape[0]
+    chunk = math.gcd(outer, 4)
     out = jax.ShapeDtypeStruct((tokens, width), BF)
     vmem = pl.BlockSpec(memory_space=pltpu.VMEM)
     hbm = pl.BlockSpec(memory_space=pl.ANY)
@@ -479,21 +509,22 @@
         out_specs=(vmem, vmem, vmem),
         scratch_shapes=[
             pltpu.VMEM((planes + 2, rows + 2, colp, channels), BF),
-            pltpu.VMEM(conv_weight.shape, BF),
+            pltpu.VMEM((3 * channels, 9 * channels), BF),
             pltpu.VMEM(dec_weight.shape, BF),
             pltpu.VMEM((channels // 128, 512, 128), F32),
-            pltpu.VMEM((8, features, channels), BF),
+            pltpu.VMEM((2, features, 4 * channels), BF),
+            pltpu.VMEM((planes * rows * colp, 9 * channels), BF),
             pltpu.VMEM((planes, rows, colp, channels), BF),
             pltpu.VMEM((height, tokp, width), BF),
             pltpu.VMEM((2, height, tokp, width), BF),
             pltpu.VMEM((3, tokens, width), BF),
             pltpu.VMEM((4, outer, tokens, width), BF),
             pltpu.VMEM((outer, 8, round_up(tokens, 128)), F32),
-            pltpu.VMEM((outer, 2, 2 * tokens, tokens), BF),
+            pltpu.VMEM((outer // chunk, 2, 2 * tokens, chunk * tokens), BF),
             pltpu.VMEM((4, 2 * tokens, width), F32),
             pltpu.VMEM((3, tokens, width), BF),
             pltpu.VMEM((3, tokens, width), BF),
-            dma((2,)),
+            dma((28,)),
             dma((8,)),
             dma((8,)),
             dma((2, height)),

time: 46 us -> 45.2 us (0.983)
  Pallas kernels: 45.2 us -> 44.4 us
    pallas_call x1, Pallas kernels: 43.7 us -> 42.8 us  [body(): pl.pallas_call(functools.partial(kernel, depth, height), out_shape=(out,...]
where the time goes in v3:
time: 45.2 us; the launch traced here: 45 us
  Pallas kernels  44.4 us (98%)
  between operations  0.64 us (1%)
    pallas_call x1, Pallas kernels, body(): pl.pallas_call(functools.partial(kernel, depth, height), out_shape=(out,...  42.8 us
    pallas_call x1, Pallas kernels, body(): pl.pallas_call(hand_over, out_shape=(out, out, out), in_specs=[vmem, vmem...  1.54 us

profile of v3, /device:TPU:0, one launch (start us, length us, event | category | flops | bytes accessed | tf_op | source)
XLA Modules:
  0.0 45.0 jit_solution(13818599716498907310)
XLA Ops:
  0.6 42.8 %shard_map.85 = (bf16[224,128]{1,0:T(8,128)(2,1)}, bf16[224,128]{1,0:T(8,128)(2,1)}, bf16[224,128]{1,0:T(8,128)(2,1)}) custom-call(bf16[224,128]{1,0:T(8,128)(2,1)} %q_ref.1, bf16[224,128]{1,0:T(8,128)(2,1)} %k_ref.1, bf16[224,128]{1,0:T(8,128)(2,1)} %v_ref.1, bf16[2,4,56,256]{3,2,1,0:T(8,128)(2,1)} %x_ref.1, bf16[3,3,3,256,256]{4,3,2,1,0:T(8,128)(2,1)} %w_hbm.1, ...), custom_call_target="tpu_custom_call" | custom-call | flops 4000000000 | bytes 8000000 | tf_op jit(solution)/shard_map/pallas_call | solution.py:505
  43.5 1.5 %shard_map.86 = (bf16[224,128]{1,0:T(8,128)(2,1)}, bf16[224,128]{1,0:T(8,128)(2,1)}, bf16[224,128]{1,0:T(8,128)(2,1)}) custom-call(bf16[224,128]{1,0:T(8,128)(2,1)} %get-tuple-element.6.a_ref, bf16[224,128]{1,0:T(8,128)(2,1)} %get-tuple-element.7.b_ref, bf16[224,128]{1,0:T(8,128)(2,1)} %get-tuple-element.8.c_ref), custom_call_target="tpu_custom_call" | custom-call | tf_op jit(solution)/shard_map/pallas_call | solution.py:548

commit v4 on v3

--- a/solution.py
+++ b/solution.py
@@ -156,13 +156,12 @@
         )
 
     sources = {KEYS: k_ref, VALUES: v_ref, QUERIES: q_ref}
-    swap_copy(KEYS).start()
     for index, (dz, dy) in enumerate(ways):
         @pl.when(exists(dz, dy))
         def _(index=index, dz=dz, dy=dy):
             halo_copy(index, dz, dy).start()
-    swap_copy(VALUES).start()
-    swap_copy(QUERIES).start()
+    for array in (KEYS, VALUES, QUERIES):
+        swap_copy(array).start()
 
     lane = lax.broadcasted_iota(jnp.int32, (tokens, width), 1)
     tall_lane = lax.broadcasted_iota(jnp.int32, (2 * tokens, width), 1)
@@ -222,7 +221,7 @@
                     lanes, pl.ds(s, part_len, stride=8), :
                 ].astype(BF)
 
-    for array in (KEYS, VALUES, QUERIES):
+    def pass_on(array):
         swap_copy(array).wait_recv()
         blocks[array, z] = merged(sources[array][...], swapped[array])
         send_own(array)
@@ -237,12 +236,15 @@
     for n, (i, j) in enumerate(taps):
         window = halo[2 - i : 2 - i + planes, 2 - j : 2 - j + rows]
         windows[:, n * channels : (n + 1) * channels] = window.reshape(flat, channels)
-    sums = dot_nt(windows[...], w_ref[...])
-    total = (
-        pltpu.roll(sums[:, :channels], flat - 1, 0)
-        + sums[:, channels : 2 * channels]
-        + pltpu.roll(sums[:, 2 * channels :], 1, 0)
-    )
+    pass_on(KEYS)
+    shifts = (flat - 1, 0, 1)
+    for l, array in enumerate((VALUES, QUERIES, None)):
+        part = dot_nt(windows[...], w_ref[l * channels : (l + 1) * channels])
+        if shifts[l]:
+            part = pltpu.roll(part, shifts[l], 0)
+        total = part if l == 0 else total + part
+        if array is not None:
+            pass_on(array)
     voxels[...] = (LOSS_SCALE * total).astype(BF).reshape(planes, rows, colp, channels)
 
     lhs = jnp.concatenate(

time: 45.2 us -> 48.5 us (1.073)
  Pallas kernels: 44.4 us -> 47.7 us
    pallas_call x1, Pallas kernels: 42.8 us -> 46.2 us  [body(): pl.pallas_call(functools.partial(kernel, depth, height), out_shape=(out,...]
where the time goes in v4:
time: 48.5 us; the launch traced here: 48.4 us
  Pallas kernels  47.7 us (98%)
  between operations  0.64 us (1%)
    pallas_call x1, Pallas kernels, body(): pl.pallas_call(functools.partial(kernel, depth, height), out_shape=(out,...  46.2 us
    pallas_call x1, Pallas kernels, body(): pl.pallas_call(hand_over, out_shape=(out, out, out), in_specs=[vmem, vmem...  1.54 us

profile of v4, /device:TPU:0, one launch (start us, length us, event | category | flops | bytes accessed | tf_op | source)
XLA Modules:
  0.0 48.4 jit_solution(1404504228328722916)
XLA Ops:
  0.6 46.2 %shard_map.85 = (bf16[224,128]{1,0:T(8,128)(2,1)}, bf16[224,128]{1,0:T(8,128)(2,1)}, bf16[224,128]{1,0:T(8,128)(2,1)}) custom-call(bf16[224,128]{1,0:T(8,128)(2,1)} %q_ref.1, bf16[224,128]{1,0:T(8,128)(2,1)} %k_ref.1, bf16[224,128]{1,0:T(8,128)(2,1)} %v_ref.1, bf16[2,4,56,256]{3,2,1,0:T(8,128)(2,1)} %x_ref.1, bf16[3,3,3,256,256]{4,3,2,1,0:T(8,128)(2,1)} %w_hbm.1, ...), custom_call_target="tpu_custom_call" | custom-call | flops 4000000000 | bytes 8000000 | tf_op jit(solution)/shard_map/pallas_call | solution.py:507
  46.8 1.5 %shard_map.86 = (bf16[224,128]{1,0:T(8,128)(2,1)}, bf16[224,128]{1,0:T(8,128)(2,1)}, bf16[224,128]{1,0:T(8,128)(2,1)}) custom-call(bf16[224,128]{1,0:T(8,128)(2,1)} %get-tuple-element.6.a_ref, bf16[224,128]{1,0:T(8,128)(2,1)} %get-tuple-element.7.b_ref, bf16[224,128]{1,0:T(8,128)(2,1)} %get-tuple-element.8.c_ref), custom_call_target="tpu_custom_call" | custom-call | tf_op jit(solution)/shard_map/pallas_call | solution.py:550

commit v5 on v3

--- a/solution.py
+++ b/solution.py
@@ -156,13 +156,12 @@
         )
 
     sources = {KEYS: k_ref, VALUES: v_ref, QUERIES: q_ref}
-    swap_copy(KEYS).start()
+    for array in (KEYS, VALUES, QUERIES):
+        swap_copy(array).start()
     for index, (dz, dy) in enumerate(ways):
         @pl.when(exists(dz, dy))
         def _(index=index, dz=dz, dy=dy):
             halo_copy(index, dz, dy).start()
-    swap_copy(VALUES).start()
-    swap_copy(QUERIES).start()
 
     lane = lax.broadcasted_iota(jnp.int32, (tokens, width), 1)
     tall_lane = lax.broadcasted_iota(jnp.int32, (2 * tokens, width), 1)
@@ -207,6 +206,11 @@
             block_wait(array, (z + step) % outer)
             return carry
         lax.fori_loop(1, outer, one, 0)
+
+    for array in (KEYS, VALUES, QUERIES):
+        swap_copy(array).wait_recv()
+        blocks[array, z] = merged(sources[array][...], swapped[array])
+        send_own(array)
 
     load_d.wait()
     features = d_raw.shape[0]
@@ -221,11 +225,6 @@
                 d_ref[s % 2, start : start + part_len, place : place + 128] = d_tall[
                     lanes, pl.ds(s, part_len, stride=8), :
                 ].astype(BF)
-
-    for array in (KEYS, VALUES, QUERIES):
-        swap_copy(array).wait_recv()
-        blocks[array, z] = merged(sources[array][...], swapped[array])
-        send_own(array)
 
     for index, (dz, dy) in enumerate(ways):
         @pl.when(exists(-dz, -dy))

time: 45.2 us -> 45.5 us (level)
  no operation moved by 1% of the time
where the time goes in v5:
time: 45.5 us; the launch traced here: 45.3 us
  Pallas kernels  44.7 us (98%)
  between operations  0.64 us (1%)
    pallas_call x1, Pallas kernels, body(): pl.pallas_call(functools.partial(kernel, depth, height), out_shape=(out,...  43.2 us
    pallas_call x1, Pallas kernels, body(): pl.pallas_call(hand_over, out_shape=(out, out, out), in_specs=[vmem, vmem...  1.54 us

profile of v5, /device:TPU:0, one launch (start us, length us, event | category | flops | bytes accessed | tf_op | source)
XLA Modules:
  0.0 45.3 jit_solution(13047819664793059416)
XLA Ops:
  0.6 43.2 %shard_map.85 = (bf16[224,128]{1,0:T(8,128)(2,1)}, bf16[224,128]{1,0:T(8,128)(2,1)}, bf16[224,128]{1,0:T(8,128)(2,1)}) custom-call(bf16[224,128]{1,0:T(8,128)(2,1)} %q_ref.1, bf16[224,128]{1,0:T(8,128)(2,1)} %k_ref.1, bf16[224,128]{1,0:T(8,128)(2,1)} %v_ref.1, bf16[2,4,56,256]{3,2,1,0:T(8,128)(2,1)} %x_ref.1, bf16[3,3,3,256,256]{4,3,2,1,0:T(8,128)(2,1)} %w_hbm.1, ...), custom_call_target="tpu_custom_call" | custom-call | flops 4000000000 | bytes 8000000 | tf_op jit(solution)/shard_map/pallas_call | solution.py:504
  43.8 1.5 %shard_map.86 = (bf16[224,128]{1,0:T(8,128)(2,1)}, bf16[224,128]{1,0:T(8,128)(2,1)}, bf16[224,128]{1,0:T(8,128)(2,1)}) custom-call(bf16[224,128]{1,0:T(8,128)(2,1)} %get-tuple-element.6.a_ref, bf16[224,128]{1,0:T(8,128)(2,1)} %get-tuple-element.7.b_ref, bf16[224,128]{1,0:T(8,128)(2,1)} %get-tuple-element.8.c_ref), custom_call_target="tpu_custom_call" | custom-call | tf_op jit(solution)/shard_map/pallas_call | solution.py:547
